TPU v7x, 32 devices: a whole 2x2x4 slice. The times are simulated.
32 devices in a mesh: parts: 2 (over y), sector: 16 (over z, x, core).
Axes of the slice: x: 2, y: 2, z: 4, core: 2. Of those that a mesh axis runs over, the one named last changes fastest.
Arguments:
- vectors: bfloat16 [2, 32, 256, 256], P(None, ('parts', 'sector')), parts along dimension 1, may hold values from -6 to 6
- left_environment_blocks: bfloat16 [32, 26, 256, 256], P(('parts', 'sector')), parts along dimension 0, may hold values from -0.375 to 0.375
- right_env: bfloat16 [32, 26, 256, 256], P(('parts', 'sector')), parts along dimension 0, may hold values from -0.078125 to 0.078125
- mpo_coef: float32 [52, 26], P('parts'), parts along dimension 0, may hold values from -6 to 6
- mpo_pattern: int32 [52, 26], P('parts'), parts along dimension 0, may hold values 0 or 1
- left_sizes: int32 [32], P('parts'), parts along dimension 0, may hold values from 64 to 256, as said below
- right_sizes: int32 [32], P('parts'), parts along dimension 0, may hold values from 64 to 256, as said below
Outputs:
- product: bfloat16 [2, 32, 256, 256], P(None, ('parts', 'sector')), parts along dimension 1
- subspace: float32 [4, 2], P('parts'), parts along dimension 0
There are 2 independent parts, one for each index of `parts`. A program takes and returns all parts, laid end to end along the dimension named above; each array names one. Nothing has to cross between parts.
Inputs may be any that keep to these rules, and one draw needn't show every extreme that they name: `left_sizes`: at least one sector has exactly 256 states and one exactly 64. `right_sizes`: at least one sector has exactly 256 states and one exactly 64.
All inputs are finite; a program needn't handle non-finite values.
Results may differ from a plain program's by a relative error of at most 0.0064.
Values may be sent and summed in bfloat16 or wider, within the bound.
A program may use at most 128 MiB of HBM per device.

v0:
```python
import jax
import jax.numpy as jnp
from jax import lax
from jax.sharding import PartitionSpec as P


def from_behind(shard, axis, by):
    size = lax.axis_size(axis)
    pairs = [(i, i + by) for i in range(size) if 0 <= i + by < size]
    return lax.ppermute(shard, axis, pairs)


def shards(
    vectors, left_environment_blocks, right_env, mpo_coef, mpo_pattern, left_sizes, right_sizes
):
    blk = vectors.shape[2]
    width = left_environment_blocks.shape[1]
    count = vectors.shape[0]
    total_sectors = lax.axis_size("sector")
    here = lax.axis_index("sector")
    coupling = mpo_coef * mpo_pattern.astype(jnp.float32)
    states = jnp.arange(blk, dtype=jnp.int32)
    partner = jnp.minimum(here + 1, total_sectors - 1)
    row_ok = states < left_sizes[here]
    col_ok = (states < right_sizes[partner]) & (here + 1 < total_sectors)
    mask = row_ok[:, None] & col_ok[None, :]
    block = vectors[:, 0]
    active_sector_mask = jnp.where(mask[None], block, jnp.zeros_like(block))
    stacked_blocks = jnp.transpose(active_sector_mask, (1, 0, 2)).reshape(blk, count * blk)
    partial_terms = jnp.dot(
        left_environment_blocks[0].reshape(width * blk, blk),
        stacked_blocks,
        preferred_element_type=jnp.float32,
    )
    partial_terms = partial_terms.reshape(width, blk, count, blk)
    mixed = jnp.einsum(
        "wu,wavc->vuac", coupling, partial_terms, precision=lax.Precision.HIGHEST
    ).astype(jnp.bfloat16)
    neighbour_env = from_behind(right_env, "sector", -1)
    matvec_output = jnp.einsum(
        "vuac,udc->vad", mixed, neighbour_env[0], preferred_element_type=jnp.float32
    ).astype(jnp.bfloat16)
    matvec_output = jnp.where(mask[None], matvec_output, jnp.zeros_like(matvec_output))
    sector_local_terms = jnp.einsum(
        "hzp,ozp->ho", active_sector_mask, matvec_output, preferred_element_type=jnp.float32
    )
    scale = 1.0 / jnp.sqrt(jnp.float32(total_sectors * blk * blk))
    subspace = lax.psum(sector_local_terms, "sector") * scale
    return (matvec_output[:, None], subspace)


def solution(mesh):
    placed = (
        P(None, ("parts", "sector"), None, None),
        P(("parts", "sector"), None, None, None),
        P(("parts", "sector"), None, None, None),
        P("parts", None),
        P("parts", None),
        P("parts"),
        P("parts"),
    )
    return jax.shard_map(
        shards,
        mesh=mesh,
        in_specs=placed,
        out_specs=(P(None, ("parts", "sector"), None, None), P("parts", None)),
        check_vma=False,
    )
```

profile of v0, /device:TPU:0, one launch (start us, length us, event | category | flops | bytes accessed | tf_op | source)
XLA Modules:
  0.0 126.3 jit_solution(8441668676584414295)
XLA Ops:
  0.6 0.0 copy-start
  0.6 1.6 %collective-permute-start = (bf16[1,26,256,256]{3,2,1,0:T(8,128)(2,1)}, bf16[1,26,256,256]{3,2,1,0:T(8,128)(2,1)}, u32[]{:S(2)}, u32[]{:S(2)}) collective-permute-start(bf16[1,26,256,256]{3,2,1,0:T(8,128)(2,1)} %param.9), channel_id=1, source_target_pairs={{1,0},{2,1},{3,2},{4,3},{5,4},{6,5},{7,6},{8,7},{9,8},{10,9},{11,1... | collective-permute-start | bytes 10223624 | tf_op jit(solution)/shard_map/ppermute | solution.py:10
  2.2 1.2 dynamic_slice.7
  3.5 1.2 dynamic_slice.6
  4.7 1.3 %compare_and_fusion = (pred[256]{0:T(512)(128)(4,1)S(1)}, pred[256]{0:T(512)(128)(4,1)S(1)}) fusion(pred[]{:T(512)S(6)} %lt.35, s32[]{:T(128)} %bitcast.1, s32[]{:T(128)} %bitcast), kind=kLoop, calls=%fused_computation.15 | loop fusion | flops 768 | bytes 521 | tf_op jit(solution)/shard_map/and | solution.py:25
  6.0 0.1 broadcast_and_fusion
  6.1 1.7 %fusion.28 = bf16[256,2,256]{2,0,1:T(8,128)(2,1)} fusion(bf16[2,1,256,256]{3,2,1,0:T(8,128)(2,1)} %param.7, pred[256,256]{1,0:T(8,128)(4,1)S(1)} %broadcast_and_fusion), kind=kLoop, calls=%fused_computation.18 | loop fusion | flops 131072 | bytes 589824 | tf_op jit(solution)/shard_map/transpose | solution.py:29
  7.8 1.8 %copy.12 = bf16[256,2,256]{0,2,1:T(8,128)(2,1)} copy(bf16[256,2,256]{2,0,1:T(8,128)(2,1)} %fusion.28) | data formatting | bytes 524288 | tf_op jit(solution)/shard_map/transpose | solution.py:29
  9.6 0.0 copy-done
  9.6 7.8 %convolution_bitcast_fusion = f32[6656,512]{0,1:T(8,128)} fusion(bf16[256,512]{0,1:T(8,128)(2,1)} %bitcast.56, bf16[6656,256]{1,0:T(8,128)(2,1)S(1)} %bitcast.55), kind=kOutput, calls=%fused_computation.1 | convolution fusion | flops 1744830464 | bytes 17301504 | tf_op jit(solution)/shard_map/dot_general | solution.py:30
  17.4 15.9 %reshape.52 = f32[26,256,2,256]{1,0,3,2:T(8,128)} reshape(f32[6656,512]{0,1:T(8,128)} %convolution_bitcast_fusion) | data formatting | bytes 27262976 | tf_op jit(solution)/shard_map/reshape | solution.py:35
  33.3 0.0 copy-start.2
  33.3 0.0 copy-start.3
  33.3 0.0 copy-start.4
  33.3 20.4 %copy.17 = f32[26,256,2,256]{3,0,2,1:T(8,128)} copy(f32[26,256,2,256]{1,0,3,2:T(8,128)} %reshape.52) | data formatting | bytes 27262976 | tf_op jit(solution)/shard_map/reshape | solution.py:35
  53.7 0.0 copy-done.2
  53.7 0.9 copy.14
  54.6 0.0 copy-done.3
  54.6 0.0 copy-done.4
  54.6 0.0 copy-start.1
  54.6 19.4 %fusion.19 = bf16[256,2,256,26]{2,3,1,0:T(8,128)(2,1)S(1)} fusion(f32[26,256,2,256]{3,0,2,1:T(8,128)} %copy.17, f32[26,26]{1,0:T(8,128)S(1)} %copy-done.3, s32[26,26]{1,0:T(8,128)S(1)} %copy-done.4), kind=kOutput, calls=%fused_computation.11 | convolution fusion | flops 1063257408 | bytes 20452640 | tf_op jit(solution)/shard_map/wu,wavc->vuac/dot_general | solution.py:36
  74.0 0.0 collective-permute-done
  74.0 10.0 %fusion.14 = bf16[2,256,256]{2,1,0:T(8,128)(2,1)} fusion(bf16[1,26,256,256]{3,2,1,0:T(8,128)(2,1)} %collective-permute-done, bf16[256,2,256,26]{2,3,1,0:T(8,128)(2,1)S(1)} %fusion.19, pred[256,256]{1,0:T(8,128)(4,1)S(1)} %broadcast_and_fusion), kind=kOutput, calls=%fused_computation.7 | convolution fusion | flops 1745092608 | bytes 10551296 | tf_op jit(solution)/shard_map/vuac,udc->vad/dot_general | solution.py:40
  84.1 1.8 %copy.15 = bf16[2,256,256]{1,0,2:T(2,128)(2,1)} copy(bf16[2,256,256]{2,1,0:T(8,128)(2,1)} %fusion.14) | data formatting | bytes 524288 | tf_op jit(solution)/shard_map/jit(_where)/select_n | solution.py:43
  85.9 1.9 %convolution_bitcast_fusion.1 = f32[2,2]{1,0:T(2,128)S(1)} fusion(bf16[2,256,256]{1,0,2:T(2,128)(2,1)} %copy.14, bf16[2,256,256]{1,0,2:T(2,128)(2,1)} %copy.15), kind=kOutput, calls=%fused_computation.8 | convolution fusion | flops 524288 | bytes 524304 | tf_op jit(solution)/shard_map/hzp,ozp->ho/dot_general | solution.py:44
  87.8 37.9 %psum.7 = f32[2,2]{1,0:T(2,128)S(1)} all-reduce(f32[2,2]{1,0:T(2,128)S(1)} %convolution_bitcast_fusion.1), channel_id=1, replica_groups=mesh['parts'=2,'sector'=16] {'sector'}, use_global_device_ids=true, to_apply=%region_0.1 | all-reduce | flops 4 | bytes 32 | tf_op jit(solution)/shard_map/psum | solution.py:48
  125.7 0.6 broadcast_multiply_fusion
  126.3 0.0 copy-done.1
  (1 shorter events, 0.0 us)
Async XLA Ops:
  0.6 8.9 %copy-start = (bf16[1,26,256,256]{3,2,1,0:T(8,128)(2,1)S(1)}, bf16[1,26,256,256]{3,2,1,0:T(8,128)(2,1)}, u32[]{:S(2)}) copy-start(bf16[1,26,256,256]{3,2,1,0:T(8,128)(2,1)} %param.8) | copy-start | bytes 10223620
  0.6 73.4 %collective-permute-start = (bf16[1,26,256,256]{3,2,1,0:T(8,128)(2,1)}, bf16[1,26,256,256]{3,2,1,0:T(8,128)(2,1)}, u32[]{:S(2)}, u32[]{:S(2)}) collective-permute-start(bf16[1,26,256,256]{3,2,1,0:T(8,128)(2,1)} %param.9), channel_id=1, source_target_pairs={{1,0},{2,1},{3,2},{4,3},{5,4},{6,5},{7,6},{8,7},{9,8},{10,9},{11,1... | collective-permute-start | bytes 10223624 | tf_op jit(solution)/shard_map/ppermute | solution.py:10
  33.3 20.4 %copy-start.2 = (bf16[2,1,256,256]{3,2,1,0:T(8,128)(2,1)S(1)}, bf16[2,1,256,256]{3,2,1,0:T(8,128)(2,1)}, u32[]{:S(2)}) copy-start(bf16[2,1,256,256]{3,2,1,0:T(8,128)(2,1)} %param.7) | copy-start | bytes 786436
  33.3 21.3 %copy-start.3 = (f32[26,26]{1,0:T(8,128)S(1)}, f32[26,26]{1,0:T(8,128)}, u32[]{:S(2)}) copy-start(f32[26,26]{1,0:T(8,128)} %param.10) | copy-start | bytes 8116
  33.3 21.3 %copy-start.4 = (s32[26,26]{1,0:T(8,128)S(1)}, s32[26,26]{1,0:T(8,128)}, u32[]{:S(2)}) copy-start(s32[26,26]{1,0:T(8,128)} %param.11) | copy-start | bytes 8116
  54.6 71.7 %copy-start.1 = (bf16[1,26,256,256]{3,2,1,0:T(8,128)(2,1)S(1)}, bf16[1,26,256,256]{3,2,1,0:T(8,128)(2,1)}, u32[]{:S(2)}) copy-start(bf16[1,26,256,256]{3,2,1,0:T(8,128)(2,1)} %param.8) | copy-start | bytes 10223620
where the time goes:
time: 127 us; the launch traced here: 126 us
  local copies, waits for them, and re-layouts  43.3 us (34%)
  matrix products  39.2 us (31%)
  blocking collectives  37.9 us (30%)
  other arithmetic  3.67 us (3%)
  starting transfers between devices  1.56 us (1%)
    psum x1, blocking collectives, shards(): subspace = lax.psum(sector_local_terms, 'sector') * scale  37.9 us
    reshape x2, local copies, waits for them, and re-layouts, shards(): partial_terms = partial_terms.reshape(width, blk, count, blk)  36.3 us
    dot_general x1, matrix products, shards(): jnp.einsum('wu,wavc->vuac', coupling, partial_terms, precision=lax.Precis...  19.4 us
    dot_general x1, matrix products, shards(): jnp.einsum('vuac,udc->vad', mixed, neighbour_env[0], preferred_element_ty...  10 us
    dot_general x1, matrix products, shards(): jnp.dot(left_environment_blocks[0].reshape(width * blk, blk), stacked_blo...  7.81 us
  transfers between devices with their start and end apart: 1, of which 0 were waited for; matrix products, arithmetic and copies ran while one was open for 57% of the time, Pallas kernels for 0%

commit v1 on v0

v1 whole, which is shorter than its diff:
```python
import functools

import jax
import jax.numpy as jnp
from jax import lax
from jax.experimental import pallas as pl
from jax.experimental.pallas import tpu as pltpu
from jax.sharding import PartitionSpec as P

MESH = pl.DeviceIdType.MESH
ROWS = 16


def kernel(
    sectors,
    group,
    left_sizes,
    right_sizes,
    coef,
    pattern,
    vectors,
    left_env,
    right_env,
    product,
    subspace,
    left,
    left_high,
    left_low,
    mixed,
    arrived,
    total,
    terms,
    gathered,
    left_sem,
    send_sem,
    recv_sem,
    term_send_sem,
    term_recv_sem,
):
    count, _, blk, _ = vectors.shape
    width = coef.shape[0]
    steps = width // group
    wide = width * ROWS
    here = lax.axis_index("sector")
    has_partner = here + 1 < sectors

    left_copy = pltpu.make_async_copy(left_env.at[0], left, left_sem)
    left_copy.start()

    barrier = pltpu.get_barrier_semaphore()

    def greet(k, carry):
        peer = lax.rem(here + k, sectors)
        pl.semaphore_signal(barrier, inc=1, device_id={"sector": peer}, device_id_type=MESH)
        return carry

    lax.fori_loop(1, sectors, greet, 0)
    pl.semaphore_wait(barrier, sectors - 1)

    def env_copy(i):
        piece = pl.ds(i * group, group)
        return pltpu.make_async_remote_copy(
            src_ref=right_env.at[0, piece],
            dst_ref=arrived.at[piece],
            send_sem=send_sem.at[i],
            recv_sem=recv_sem.at[i],
            device_id={"sector": lax.rem(here + sectors - 1, sectors)},
            device_id_type=MESH,
        )

    @pl.when(here > 0)
    def _():
        def send(i, carry):
            env_copy(i).start()
            return carry

        lax.fori_loop(0, steps, send, 0)

    partner = jnp.minimum(here + 1, sectors - 1)
    row_limit = left_sizes[here]
    col_limit = jnp.where(has_partner, right_sizes[partner], 0)
    rows = lax.broadcasted_iota(jnp.int32, (blk, blk), 0)
    cols = lax.broadcasted_iota(jnp.int32, (blk, blk), 1)
    mask = (rows < row_limit) & (cols < col_limit)
    live = [
        jnp.where(mask, vectors[v, 0].astype(jnp.float32), 0.0).astype(jnp.bfloat16)
        for v in range(count)
    ]
    live_wide = jnp.concatenate(live, axis=1)

    coupling = coef[...] * pattern[...].astype(jnp.float32)
    high = coupling.astype(jnp.bfloat16)
    low = (coupling - high.astype(jnp.float32)).astype(jnp.bfloat16)
    pick_rows = (
        lax.broadcasted_iota(jnp.int32, (wide, width), 0) // ROWS
        == lax.broadcasted_iota(jnp.int32, (wide, width), 1)
    ).astype(jnp.float32).astype(jnp.bfloat16)
    pick_cols = (
        lax.broadcasted_iota(jnp.int32, (width, wide), 1) // ROWS
        == lax.broadcasted_iota(jnp.int32, (width, wide), 0)
    ).astype(jnp.float32).astype(jnp.bfloat16)
    same = (
        lax.broadcasted_iota(jnp.int32, (wide, wide), 0) % ROWS
        == lax.broadcasted_iota(jnp.int32, (wide, wide), 1) % ROWS
    )

    def spread(part):
        tall = lax.dot_general(
            pick_rows, part, (((1,), (1,)), ((), ())), preferred_element_type=jnp.float32
        ).astype(jnp.bfloat16)
        full = jnp.dot(tall, pick_cols, preferred_element_type=jnp.float32)
        return jnp.where(same, full, 0.0).astype(jnp.bfloat16)

    spread_high = spread(high)
    spread_low = spread(low)

    left_copy.wait()

    def mix_rows(g, carry):
        piece = pl.ds(pl.multiple_of(g * ROWS, ROWS), ROWS)
        block = left[:, piece, :].reshape(wide, blk)
        out = jnp.dot(spread_high, block, preferred_element_type=jnp.float32) + jnp.dot(
            spread_low, block, preferred_element_type=jnp.float32
        )
        out_high = out.astype(jnp.bfloat16)
        out_low = (out - out_high.astype(jnp.float32)).astype(jnp.bfloat16)
        left_high[:, piece, :] = out_high.reshape(width, ROWS, blk)
        left_low[:, piece, :] = out_low.reshape(width, ROWS, blk)
        return carry

    lax.fori_loop(0, blk // ROWS, mix_rows, 0)

    def apply_left(u, carry):
        out = jnp.dot(left_high[u], live_wide, preferred_element_type=jnp.float32) + jnp.dot(
            left_low[u], live_wide, preferred_element_type=jnp.float32
        )
        out = out.astype(jnp.bfloat16)
        for v in range(count):
            mixed[u, pl.ds(v * blk, blk), :] = out[:, v * blk : (v + 1) * blk]
        return carry

    lax.fori_loop(0, width, apply_left, 0)

    total[...] = jnp.zeros_like(total)

    @pl.when(has_partner)
    def _():
        def apply_right(i, carry):
            env_copy(i).wait_recv()
            out = total[...]
            for j in range(group):
                u = i * group + j
                out += lax.dot_general(
                    mixed[u],
                    arrived[u],
                    (((1,), (1,)), ((), ())),
                    preferred_element_type=jnp.float32,
                )
            total[...] = out
            return carry

        lax.fori_loop(0, steps, apply_right, 0)

    terms[...] = jnp.zeros_like(terms)
    lanes = terms.shape[1]
    for j in range(count):
        block = jnp.where(mask, total[pl.ds(j * blk, blk), :], 0.0).astype(jnp.bfloat16)
        product[j, 0] = block
        block = block.astype(jnp.float32)
        for i in range(count):
            line = jnp.sum(live[i].astype(jnp.float32) * block, axis=0, keepdims=True)
            short = line[:, :lanes]
            for part in range(1, blk // lanes):
                short = short + line[:, part * lanes : (part + 1) * lanes]
            row = i * count + j
            terms[row : row + 1, :] = short

    gathered[here] = terms[...]

    def term_copy(k):
        return pltpu.make_async_remote_copy(
            src_ref=terms,
            dst_ref=gathered.at[here],
            send_sem=term_send_sem.at[k],
            recv_sem=term_recv_sem.at[k],
            device_id={"sector": lax.rem(here + k, sectors)},
            device_id_type=MESH,
        )

    def send_terms(k, carry):
        term_copy(k).start()
        return carry

    def wait_terms(k, carry):
        term_copy(k).wait_recv()
        return carry

    def wait_terms_sent(k, carry):
        term_copy(k).wait_send()
        return carry

    lax.fori_loop(1, sectors, send_terms, 0)
    lax.fori_loop(1, sectors, wait_terms, 0)

    summed = gathered[0]
    for s in range(1, sectors):
        summed = summed + gathered[s]
    scale = 1.0 / jnp.sqrt(jnp.float32(sectors * blk * blk))
    sums = jnp.sum(summed, axis=1, keepdims=True) * scale
    out_rows = lax.broadcasted_iota(jnp.int32, (count, count), 0)
    out_cols = lax.broadcasted_iota(jnp.int32, (count, count), 1)
    result = jnp.zeros((count, count), jnp.float32)
    for i in range(count):
        for j in range(count):
            row = i * count + j
            value = jnp.broadcast_to(sums[row : row + 1, :], (count, count))
            result = jnp.where((out_rows == i) & (out_cols == j), value, result)
    subspace[...] = result

    lax.fori_loop(1, sectors, wait_terms_sent, 0)

    @pl.when(here > 0)
    def _():
        def sent(i, carry):
            env_copy(i).wait_send()
            return carry

        lax.fori_loop(0, steps, sent, 0)


def shards(
    vectors, left_environment_blocks, right_env, mpo_coef, mpo_pattern, left_sizes, right_sizes
):
    count, _, blk, _ = vectors.shape
    width = left_environment_blocks.shape[1]
    sectors = lax.axis_size("sector")
    group = 2 if width % 2 == 0 else 1
    steps = width // group
    tile_rows = -(-count * count // 8) * 8
    vmem = pl.BlockSpec(memory_space=pltpu.VMEM)
    smem = pl.BlockSpec(memory_space=pltpu.SMEM)
    hbm = pl.BlockSpec(memory_space=pl.ANY)
    return pl.pallas_call(
        functools.partial(kernel, sectors, group),
        out_shape=(
            jax.ShapeDtypeStruct(vectors.shape, jnp.bfloat16),
            jax.ShapeDtypeStruct((count, count), jnp.float32),
        ),
        in_specs=[smem, smem, vmem, vmem, vmem, hbm, hbm],
        out_specs=(vmem, vmem),
        scratch_shapes=[
            pltpu.VMEM((width, blk, blk), jnp.bfloat16),
            pltpu.VMEM((width, blk, blk), jnp.bfloat16),
            pltpu.VMEM((width, blk, blk), jnp.bfloat16),
            pltpu.VMEM((width, count * blk, blk), jnp.bfloat16),
            pltpu.VMEM((width, blk, blk), jnp.bfloat16),
            pltpu.VMEM((count * blk, blk), jnp.float32),
            pltpu.VMEM((tile_rows, 128), jnp.float32),
            pltpu.VMEM((sectors, tile_rows, 128), jnp.float32),
            pltpu.SemaphoreType.DMA,
            pltpu.SemaphoreType.DMA((steps,)),
            pltpu.SemaphoreType.DMA((steps,)),
            pltpu.SemaphoreType.DMA((sectors,)),
            pltpu.SemaphoreType.DMA((sectors,)),
        ],
        compiler_params=pltpu.CompilerParams(
            collective_id=0, has_side_effects=True, vmem_limit_bytes=48 * 1024 * 1024
        ),
        cost_estimate=pl.CostEstimate(
            flops=4 * width * blk * blk * blk * count,
            bytes_accessed=3 * width * blk * blk * 2,
            transcendentals=0,
        ),
    )(
        left_sizes,
        right_sizes,
        mpo_coef,
        mpo_pattern,
        vectors,
        left_environment_blocks,
        right_env,
    )


def solution(mesh):
    placed = (
        P(None, ("parts", "sector"), None, None),
        P(("parts", "sector"), None, None, None),
        P(("parts", "sector"), None, None, None),
        P("parts", None),
        P("parts", None),
        P("parts"),
        P("parts"),
    )
    return jax.shard_map(
        shards,
        mesh=mesh,
        in_specs=placed,
        out_specs=(P(None, ("parts", "sector"), None, None), P("parts", None)),
        check_vma=False,
    )
```

time: 127 us -> 57.6 us (0.45)
  Pallas kernels: 0 us -> 49.6 us
  matrix products: 39.2 us -> 0 us
  blocking collectives: 37.9 us -> 0 us
  local copies, waits for them, and re-layouts: 43.3 us -> 6.92 us
  other arithmetic: 3.67 us -> 0 us
  starting transfers between devices: 1.56 us -> 0 us
    pallas_call x0 -> x1, Pallas kernels: none -> 49.6 us  [shards(): pl.pallas_call(functools.partial(kernel, sectors, group), out_shape=(jax....]
    dot_general x4 -> x0, matrix products: 39.2 us -> none  [the longest x1 19.4 us: shards(): jnp.einsum('wu,wavc->vuac', coupling, partial_terms, precision=lax.Precis...]
    psum x1 -> x0, blocking collectives: 37.9 us -> none  [shards(): subspace = lax.psum(sector_local_terms, 'sector') * scale]
    reshape x2 -> x0, local copies, waits for them, and re-layouts: 36.3 us -> none  [shards(): partial_terms = partial_terms.reshape(width, blk, count, blk)]
    unnamed x10 -> x14, local copies, waits for them, and re-layouts: 0.03 us -> 6.92 us
    select_n x2 -> x0, local copies, waits for them, and re-layouts: 2.67 us -> none  [the longest x1 1.81 us: shards(): jnp.where(mask[None], matvec_output, jnp.zeros_like(matvec_output))]
    dynamic_slice x2 -> x0, local copies, waits for them, and re-layouts: 2.48 us -> none  [the longest x1 1.24 us: shards(): col_ok = (states < right_sizes[partner]) & (here + 1 < total_sectors)]
    transpose x1 -> x0, local copies, waits for them, and re-layouts: 1.78 us -> none  [shards(): jnp.transpose(active_sector_mask, (1, 0, 2)).reshape(blk, count * blk)]
  transfers between devices with their start and end apart: 1 -> 0, of which waited for: 0 -> 0; matrix products, arithmetic and copies ran while one was open for 57% -> 0% of each run, Pallas kernels for 0% -> 0%
where the time goes in v1:
time: 57.6 us; the launch traced here: 57.2 us
  Pallas kernels  49.6 us (86%)
  local copies, waits for them, and re-layouts  6.92 us (12%)
  between operations  0.65 us (1%)
    pallas_call x1, Pallas kernels, shards(): pl.pallas_call(functools.partial(kernel, sectors, group), out_shape=(jax....  49.6 us
    unnamed x14, local copies, waits for them, and re-layouts  6.92 us

profile of v1, /device:TPU:0, one launch (start us, length us, event | category | flops | bytes accessed | tf_op | source)
XLA Modules:
  0.0 57.2 jit_solution(17086979157789166762)
XLA Ops:
  0.6 0.0 copy-start
  0.6 2.0 %copy-done = bf16[1,26,256,256]{3,2,1,0:T(8,128)(2,1)S(1)} copy-done((bf16[1,26,256,256]{3,2,1,0:T(8,128)(2,1)S(1)}, bf16[1,26,256,256]{3,2,1,0:T(8,128)(2,1)}, u32[]{:S(2)}) %copy-start) | copy-done | bytes 3407896
  2.6 0.0 copy-start.1
  2.6 0.9 %copy-done.1 = bf16[2,1,256,256]{3,2,1,0:T(8,128)(2,1)S(1)} copy-done((bf16[2,1,256,256]{3,2,1,0:T(8,128)(2,1)S(1)}, bf16[2,1,256,256]{3,2,1,0:T(8,128)(2,1)}, u32[]{:S(2)}) %copy-start.1) | copy-done | bytes 262168
  3.5 0.0 copy-start.2
  3.5 0.7 %copy-done.2 = f32[26,26]{1,0:T(8,128)S(1)} copy-done((f32[26,26]{1,0:T(8,128)S(1)}, f32[26,26]{1,0:T(8,128)}, u32[]{:S(2)}) %copy-start.2) | copy-done | bytes 2728
  4.3 0.0 copy-start.3
  4.3 0.7 %copy-done.3 = s32[26,26]{1,0:T(8,128)S(1)} copy-done((s32[26,26]{1,0:T(8,128)S(1)}, s32[26,26]{1,0:T(8,128)}, u32[]{:S(2)}) %copy-start.3) | copy-done | bytes 2728
  5.0 0.0 copy-start.4
  5.0 0.7 %copy-done.4 = s32[16]{0:T(128)S(1)} copy-done((s32[16]{0:T(128)S(1)}, s32[16]{0:T(128)}, u32[]{:S(2)}) %copy-start.4) | copy-done | bytes 88
  5.6 0.0 copy-start.5
  5.6 0.7 %copy-done.5 = s32[16]{0:T(128)S(1)} copy-done((s32[16]{0:T(128)S(1)}, s32[16]{0:T(128)}, u32[]{:S(2)}) %copy-start.5) | copy-done | bytes 88
  6.3 49.6 %shard_map.86 = (bf16[2,1,256,256]{3,2,1,0:T(8,128)(2,1)S(1)}, f32[2,2]{1,0:T(2,128)S(1)}) custom-call(s32[16]{0:T(128)S(1)} %copy-done.4, s32[16]{0:T(128)S(1)} %copy-done.5, f32[26,26]{1,0:T(8,128)S(1)} %copy-done.2, s32[26,26]{1,0:T(8,128)S(1)} %copy-done.3, bf16[2,1,256,256]{3,2,1,0:T(8,128)(2,1)S(1)} %copy-done.1, ...), custom_call_target="tpu_custom_call" | custom-call | flops 3489660928 | bytes 10223616 | tf_op jit(solution)/shard_map/pallas_call | solution.py:243
  55.9 0.7 %copy.11 = bf16[2,1,256,256]{3,2,1,0:T(8,128)(2,1)} copy(bf16[2,1,256,256]{3,2,1,0:T(8,128)(2,1)S(1)} %get-tuple-element.4) | data formatting | bytes 524288
  56.7 0.6 copy.12
Async XLA Ops:
  0.6 2.0 %copy-start = (bf16[1,26,256,256]{3,2,1,0:T(8,128)(2,1)S(1)}, bf16[1,26,256,256]{3,2,1,0:T(8,128)(2,1)}, u32[]{:S(2)}) copy-start(bf16[1,26,256,256]{3,2,1,0:T(8,128)(2,1)} %left_env.1) | copy-start | bytes 10223620
  2.6 0.9 %copy-start.1 = (bf16[2,1,256,256]{3,2,1,0:T(8,128)(2,1)S(1)}, bf16[2,1,256,256]{3,2,1,0:T(8,128)(2,1)}, u32[]{:S(2)}) copy-start(bf16[2,1,256,256]{3,2,1,0:T(8,128)(2,1)} %vectors.1) | copy-start | bytes 786436
  3.5 0.7 %copy-start.2 = (f32[26,26]{1,0:T(8,128)S(1)}, f32[26,26]{1,0:T(8,128)}, u32[]{:S(2)}) copy-start(f32[26,26]{1,0:T(8,128)} %coef.1) | copy-start | bytes 8116
  4.3 0.7 %copy-start.3 = (s32[26,26]{1,0:T(8,128)S(1)}, s32[26,26]{1,0:T(8,128)}, u32[]{:S(2)}) copy-start(s32[26,26]{1,0:T(8,128)} %pattern.1) | copy-start | bytes 8116
  5.0 0.7 %copy-start.4 = (s32[16]{0:T(128)S(1)}, s32[16]{0:T(128)}, u32[]{:S(2)}) copy-start(s32[16]{0:T(128)} %left_sizes.1) | copy-start | bytes 196
  5.6 0.7 %copy-start.5 = (s32[16]{0:T(128)S(1)}, s32[16]{0:T(128)}, u32[]{:S(2)}) copy-start(s32[16]{0:T(128)} %right_sizes.1) | copy-start | bytes 196

commit v2 on v1

--- a/solution.py
+++ b/solution.py
@@ -14,15 +14,20 @@
 def kernel(
     sectors,
     group,
+    left_sizes_in,
+    right_sizes_in,
+    coef_in,
+    pattern_in,
+    vectors_in,
+    left_env,
+    right_env,
+    product,
+    subspace,
     left_sizes,
     right_sizes,
     coef,
     pattern,
     vectors,
-    left_env,
-    right_env,
-    product,
-    subspace,
     left,
     left_high,
     left_low,
@@ -31,6 +36,7 @@
     total,
     terms,
     gathered,
+    small_sem,
     left_sem,
     send_sem,
     recv_sem,
@@ -44,9 +50,6 @@
     here = lax.axis_index("sector")
     has_partner = here + 1 < sectors
 
-    left_copy = pltpu.make_async_copy(left_env.at[0], left, left_sem)
-    left_copy.start()
-
     barrier = pltpu.get_barrier_semaphore()
 
     def greet(k, carry):
@@ -55,6 +58,21 @@
         return carry
 
     lax.fori_loop(1, sectors, greet, 0)
+
+    left_copy = pltpu.make_async_copy(left_env.at[0], left, left_sem)
+    small = (
+        (left_sizes_in, left_sizes),
+        (right_sizes_in, right_sizes),
+        (coef_in, coef),
+        (pattern_in, pattern),
+        (vectors_in, vectors),
+    )
+    small_copies = [
+        pltpu.make_async_copy(src, dst, small_sem.at[i]) for i, (src, dst) in enumerate(small)
+    ]
+    for copy in small_copies:
+        copy.start()
+    left_copy.start()
     pl.semaphore_wait(barrier, sectors - 1)
 
     def env_copy(i):
@@ -75,6 +93,9 @@
             return carry
 
         lax.fori_loop(0, steps, send, 0)
+
+    for copy in small_copies:
+        copy.wait()
 
     partner = jnp.minimum(here + 1, sectors - 1)
     row_limit = left_sizes[here]
@@ -238,17 +259,21 @@
     steps = width // group
     tile_rows = -(-count * count // 8) * 8
     vmem = pl.BlockSpec(memory_space=pltpu.VMEM)
-    smem = pl.BlockSpec(memory_space=pltpu.SMEM)
-    hbm = pl.BlockSpec(memory_space=pl.ANY)
+    hbm = pl.BlockSpec(memory_space=pltpu.HBM)
     return pl.pallas_call(
         functools.partial(kernel, sectors, group),
         out_shape=(
             jax.ShapeDtypeStruct(vectors.shape, jnp.bfloat16),
             jax.ShapeDtypeStruct((count, count), jnp.float32),
         ),
-        in_specs=[smem, smem, vmem, vmem, vmem, hbm, hbm],
+        in_specs=[hbm] * 7,
         out_specs=(vmem, vmem),
         scratch_shapes=[
+            pltpu.SMEM(left_sizes.shape, jnp.int32),
+            pltpu.SMEM(right_sizes.shape, jnp.int32),
+            pltpu.VMEM(mpo_coef.shape, jnp.float32),
+            pltpu.VMEM(mpo_pattern.shape, jnp.int32),
+            pltpu.VMEM(vectors.shape, jnp.bfloat16),
             pltpu.VMEM((width, blk, blk), jnp.bfloat16),
             pltpu.VMEM((width, blk, blk), jnp.bfloat16),
             pltpu.VMEM((width, blk, blk), jnp.bfloat16),
@@ -257,6 +282,7 @@
             pltpu.VMEM((count * blk, blk), jnp.float32),
             pltpu.VMEM((tile_rows, 128), jnp.float32),
             pltpu.VMEM((sectors, tile_rows, 128), jnp.float32),
+            pltpu.SemaphoreType.DMA((5,)),
             pltpu.SemaphoreType.DMA,
             pltpu.SemaphoreType.DMA((steps,)),
             pltpu.SemaphoreType.DMA((steps,)),

time: 57.6 us -> 56.8 us (0.986)
  Pallas kernels: 49.6 us -> 48.8 us
    pallas_call x1, Pallas kernels: 49.6 us -> 48.8 us  [shards(): pl.pallas_call(functools.partial(kernel, sectors, group), out_shape=(jax....]
where the time goes in v2:
time: 56.8 us; the launch traced here: 56.4 us
  Pallas kernels  48.8 us (86%)
  local copies, waits for them, and re-layouts  6.92 us (12%)
  between operations  0.65 us (1%)
    pallas_call x1, Pallas kernels, shards(): pl.pallas_call(functools.partial(kernel, sectors, group), out_shape=(jax....  48.8 us
    unnamed x14, local copies, waits for them, and re-layouts  6.92 us

profile of v2, /device:TPU:0, one launch (start us, length us, event | category | flops | bytes accessed | tf_op | source)
XLA Modules:
  0.0 56.4 jit_solution(5835889736110089436)
XLA Ops:
  0.6 0.0 copy-start
  0.6 2.0 %copy-done = bf16[1,26,256,256]{3,2,1,0:T(8,128)(2,1)S(1)} copy-done((bf16[1,26,256,256]{3,2,1,0:T(8,128)(2,1)S(1)}, bf16[1,26,256,256]{3,2,1,0:T(8,128)(2,1)}, u32[]{:S(2)}) %copy-start) | copy-done | bytes 3407896
  2.6 0.0 copy-start.1
  2.6 0.9 %copy-done.1 = bf16[2,1,256,256]{3,2,1,0:T(8,128)(2,1)S(1)} copy-done((bf16[2,1,256,256]{3,2,1,0:T(8,128)(2,1)S(1)}, bf16[2,1,256,256]{3,2,1,0:T(8,128)(2,1)}, u32[]{:S(2)}) %copy-start.1) | copy-done | bytes 262168
  3.5 0.0 copy-start.2
  3.5 0.7 %copy-done.2 = f32[26,26]{1,0:T(8,128)S(1)} copy-done((f32[26,26]{1,0:T(8,128)S(1)}, f32[26,26]{1,0:T(8,128)}, u32[]{:S(2)}) %copy-start.2) | copy-done | bytes 2728
  4.3 0.0 copy-start.3
  4.3 0.7 %copy-done.3 = s32[26,26]{1,0:T(8,128)S(1)} copy-done((s32[26,26]{1,0:T(8,128)S(1)}, s32[26,26]{1,0:T(8,128)}, u32[]{:S(2)}) %copy-start.3) | copy-done | bytes 2728
  5.0 0.0 copy-start.4
  5.0 0.7 %copy-done.4 = s32[16]{0:T(128)S(1)} copy-done((s32[16]{0:T(128)S(1)}, s32[16]{0:T(128)}, u32[]{:S(2)}) %copy-start.4) | copy-done | bytes 88
  5.6 0.0 copy-start.5
  5.6 0.7 %copy-done.5 = s32[16]{0:T(128)S(1)} copy-done((s32[16]{0:T(128)S(1)}, s32[16]{0:T(128)}, u32[]{:S(2)}) %copy-start.5) | copy-done | bytes 88
  6.3 48.8 %shard_map.86 = (bf16[2,1,256,256]{3,2,1,0:T(8,128)(2,1)S(1)}, f32[2,2]{1,0:T(2,128)S(1)}) custom-call(s32[16]{0:T(128)S(1)} %copy-done.4, s32[16]{0:T(128)S(1)} %copy-done.5, f32[26,26]{1,0:T(8,128)S(1)} %copy-done.2, s32[26,26]{1,0:T(8,128)S(1)} %copy-done.3, bf16[2,1,256,256]{3,2,1,0:T(8,128)(2,1)S(1)} %copy-done.1, ...), custom_call_target="tpu_custom_call" | custom-call | flops 3489660928 | bytes 10223616 | tf_op jit(solution)/shard_map/pallas_call | solution.py:263
  55.1 0.7 %copy.11 = bf16[2,1,256,256]{3,2,1,0:T(8,128)(2,1)} copy(bf16[2,1,256,256]{3,2,1,0:T(8,128)(2,1)S(1)} %get-tuple-element.4) | data formatting | bytes 524288
  55.8 0.6 copy.12
Async XLA Ops:
  0.6 2.0 %copy-start = (bf16[1,26,256,256]{3,2,1,0:T(8,128)(2,1)S(1)}, bf16[1,26,256,256]{3,2,1,0:T(8,128)(2,1)}, u32[]{:S(2)}) copy-start(bf16[1,26,256,256]{3,2,1,0:T(8,128)(2,1)} %left_env.1) | copy-start | bytes 10223620
  2.6 0.9 %copy-start.1 = (bf16[2,1,256,256]{3,2,1,0:T(8,128)(2,1)S(1)}, bf16[2,1,256,256]{3,2,1,0:T(8,128)(2,1)}, u32[]{:S(2)}) copy-start(bf16[2,1,256,256]{3,2,1,0:T(8,128)(2,1)} %vectors_in.1) | copy-start | bytes 786436
  3.5 0.7 %copy-start.2 = (f32[26,26]{1,0:T(8,128)S(1)}, f32[26,26]{1,0:T(8,128)}, u32[]{:S(2)}) copy-start(f32[26,26]{1,0:T(8,128)} %coef_in.1) | copy-start | bytes 8116
  4.3 0.7 %copy-start.3 = (s32[26,26]{1,0:T(8,128)S(1)}, s32[26,26]{1,0:T(8,128)}, u32[]{:S(2)}) copy-start(s32[26,26]{1,0:T(8,128)} %pattern_in.1) | copy-start | bytes 8116
  5.0 0.7 %copy-start.4 = (s32[16]{0:T(128)S(1)}, s32[16]{0:T(128)}, u32[]{:S(2)}) copy-start(s32[16]{0:T(128)} %left_sizes_in.1) | copy-start | bytes 196
  5.6 0.7 %copy-start.5 = (s32[16]{0:T(128)S(1)}, s32[16]{0:T(128)}, u32[]{:S(2)}) copy-start(s32[16]{0:T(128)} %right_sizes_in.1) | copy-start | bytes 196

commit v3 on v2

--- a/solution.py
+++ b/solution.py
@@ -28,6 +28,7 @@
     coef,
     pattern,
     vectors,
+    result_block,
     left,
     left_high,
     left_low,
@@ -184,10 +185,12 @@
 
     terms[...] = jnp.zeros_like(terms)
     lanes = terms.shape[1]
+    blocks = [
+        jnp.where(mask, total[pl.ds(j * blk, blk), :], 0.0).astype(jnp.bfloat16)
+        for j in range(count)
+    ]
     for j in range(count):
-        block = jnp.where(mask, total[pl.ds(j * blk, blk), :], 0.0).astype(jnp.bfloat16)
-        product[j, 0] = block
-        block = block.astype(jnp.float32)
+        block = blocks[j].astype(jnp.float32)
         for i in range(count):
             line = jnp.sum(live[i].astype(jnp.float32) * block, axis=0, keepdims=True)
             short = line[:, :lanes]
@@ -195,8 +198,6 @@
                 short = short + line[:, part * lanes : (part + 1) * lanes]
             row = i * count + j
             terms[row : row + 1, :] = short
-
-    gathered[here] = terms[...]
 
     def term_copy(k):
         return pltpu.make_async_remote_copy(
@@ -221,6 +222,11 @@
         return carry
 
     lax.fori_loop(1, sectors, send_terms, 0)
+    gathered[here] = terms[...]
+    for j in range(count):
+        result_block[j, 0] = blocks[j]
+    product_copy = pltpu.make_async_copy(result_block, product, left_sem)
+    product_copy.start()
     lax.fori_loop(1, sectors, wait_terms, 0)
 
     summed = gathered[0]
@@ -237,6 +243,7 @@
             value = jnp.broadcast_to(sums[row : row + 1, :], (count, count))
             result = jnp.where((out_rows == i) & (out_cols == j), value, result)
     subspace[...] = result
+    product_copy.wait()
 
     lax.fori_loop(1, sectors, wait_terms_sent, 0)
 
@@ -247,6 +254,15 @@
             return carry
 
         lax.fori_loop(0, steps, sent, 0)
+
+
+def finish(product_in, subspace_in, product, subspace, sem):
+    first = pltpu.make_async_copy(product_in, product, sem.at[0])
+    second = pltpu.make_async_copy(subspace_in, subspace, sem.at[1])
+    first.start()
+    second.start()
+    first.wait()
+    second.wait()
 
 
 def shards(
@@ -260,19 +276,20 @@
     tile_rows = -(-count * count // 8) * 8
     vmem = pl.BlockSpec(memory_space=pltpu.VMEM)
     hbm = pl.BlockSpec(memory_space=pltpu.HBM)
-    return pl.pallas_call(
+    product, subspace = pl.pallas_call(
         functools.partial(kernel, sectors, group),
         out_shape=(
             jax.ShapeDtypeStruct(vectors.shape, jnp.bfloat16),
             jax.ShapeDtypeStruct((count, count), jnp.float32),
         ),
         in_specs=[hbm] * 7,
-        out_specs=(vmem, vmem),
+        out_specs=(hbm, vmem),
         scratch_shapes=[
             pltpu.SMEM(left_sizes.shape, jnp.int32),
             pltpu.SMEM(right_sizes.shape, jnp.int32),
             pltpu.VMEM(mpo_coef.shape, jnp.float32),
             pltpu.VMEM(mpo_pattern.shape, jnp.int32),
+            pltpu.VMEM(vectors.shape, jnp.bfloat16),
             pltpu.VMEM(vectors.shape, jnp.bfloat16),
             pltpu.VMEM((width, blk, blk), jnp.bfloat16),
             pltpu.VMEM((width, blk, blk), jnp.bfloat16),
@@ -290,7 +307,7 @@
             pltpu.SemaphoreType.DMA((sectors,)),
         ],
         compiler_params=pltpu.CompilerParams(
-            collective_id=0, has_side_effects=True, vmem_limit_bytes=48 * 1024 * 1024
+            collective_id=0, has_side_effects=True, vmem_limit_bytes=60 * 1024 * 1024
         ),
         cost_estimate=pl.CostEstimate(
             flops=4 * width * blk * blk * blk * count,
@@ -306,6 +323,16 @@
         left_environment_blocks,
         right_env,
     )
+    return pl.pallas_call(
+        finish,
+        out_shape=(
+            jax.ShapeDtypeStruct(product.shape, product.dtype),
+            jax.ShapeDtypeStruct(subspace.shape, subspace.dtype),
+        ),
+        in_specs=[vmem, vmem],
+        out_specs=(hbm, hbm),
+        scratch_shapes=[pltpu.SemaphoreType.DMA((2,))],
+    )(product, subspace)
 
 
 def solution(mesh):

time: 56.8 us -> 52 us (0.915)
  local copies, waits for them, and re-layouts: 6.92 us -> 0 us
  Pallas kernels: 48.8 us -> 51.2 us
    unnamed x14 -> x0, local copies, waits for them, and re-layouts: 6.92 us -> none
    pallas_call x0 -> x1, Pallas kernels: none -> 1.67 us  [shards(): pl.pallas_call(finish, out_shape=(jax.ShapeDtypeStruct(product.shape, pro...]
    pallas_call x1, Pallas kernels: 48.8 us -> 49.5 us  [shards(): pl.pallas_call(functools.partial(kernel, sectors, group), out_shape=(jax....]
where the time goes in v3:
time: 52 us; the launch traced here: 51.8 us
  Pallas kernels  51.2 us (98%)
  between operations  0.64 us (1%)
    pallas_call x1, Pallas kernels, shards(): pl.pallas_call(functools.partial(kernel, sectors, group), out_shape=(jax....  49.5 us
    pallas_call x1, Pallas kernels, shards(): pl.pallas_call(finish, out_shape=(jax.ShapeDtypeStruct(product.shape, pro...  1.67 us

profile of v3, /device:TPU:0, one launch (start us, length us, event | category | flops | bytes accessed | tf_op | source)
XLA Modules:
  0.0 51.8 jit_solution(14951519663237469991)
XLA Ops:
  0.6 49.5 %shard_map.86 = (bf16[2,1,256,256]{3,2,1,0:T(8,128)(2,1)}, f32[2,2]{1,0:T(2,128)}) custom-call(s32[16]{0:T(128)} %left_sizes_in.1, s32[16]{0:T(128)} %right_sizes_in.1, f32[26,26]{1,0:T(8,128)} %coef_in.1, s32[26,26]{1,0:T(8,128)} %pattern_in.1, bf16[2,1,256,256]{3,2,1,0:T(8,128)(2,1)} %vectors_in.1, bf16[1,26,256,256]{3,2,1,0:T(8,128)(2,1)} %left_env.1, ...), custom_call_target="tpu_custom_call" | custom-call | flops 3489660928 | bytes 10223616 | tf_op jit(solution)/shard_map/pallas_call | solution.py:279
  50.1 1.7 %shard_map.87 = (bf16[2,1,256,256]{3,2,1,0:T(8,128)(2,1)}, f32[2,2]{1,0:T(2,128)}) custom-call(bf16[2,1,256,256]{3,2,1,0:T(8,128)(2,1)} %get-tuple-element.4.product_in, f32[2,2]{1,0:T(2,128)} %get-tuple-element.5.subspace_in), custom_call_target="tpu_custom_call" | custom-call | tf_op jit(solution)/shard_map/pallas_call | solution.py:326

commit v4 on v3

--- a/solution.py
+++ b/solution.py
@@ -46,7 +46,6 @@
 ):
     count, _, blk, _ = vectors.shape
     width = coef.shape[0]
-    steps = width // group
     wide = width * ROWS
     here = lax.axis_index("sector")
     has_partner = here + 1 < sectors
@@ -77,7 +76,7 @@
     pl.semaphore_wait(barrier, sectors - 1)
 
     def env_copy(i):
-        piece = pl.ds(i * group, group)
+        piece = pl.ds(*group[i])
         return pltpu.make_async_remote_copy(
             src_ref=right_env.at[0, piece],
             dst_ref=arrived.at[piece],
@@ -89,11 +88,8 @@
 
     @pl.when(here > 0)
     def _():
-        def send(i, carry):
+        for i in range(len(group)):
             env_copy(i).start()
-            return carry
-
-        lax.fori_loop(0, steps, send, 0)
 
     for copy in small_copies:
         copy.wait()
@@ -167,21 +163,15 @@
 
     @pl.when(has_partner)
     def _():
-        def apply_right(i, carry):
+        def apply_right(u, carry):
+            total[...] += lax.dot_general(
+                mixed[u], arrived[u], (((1,), (1,)), ((), ())), preferred_element_type=jnp.float32
+            )
+            return carry
+
+        for i, (first, size) in enumerate(group):
             env_copy(i).wait_recv()
-            out = total[...]
-            for j in range(group):
-                u = i * group + j
-                out += lax.dot_general(
-                    mixed[u],
-                    arrived[u],
-                    (((1,), (1,)), ((), ())),
-                    preferred_element_type=jnp.float32,
-                )
-            total[...] = out
-            return carry
-
-        lax.fori_loop(0, steps, apply_right, 0)
+            lax.fori_loop(first, first + size, apply_right, 0)
 
     terms[...] = jnp.zeros_like(terms)
     lanes = terms.shape[1]
@@ -249,11 +239,8 @@
 
     @pl.when(here > 0)
     def _():
-        def sent(i, carry):
+        for i in range(len(group)):
             env_copy(i).wait_send()
-            return carry
-
-        lax.fori_loop(0, steps, sent, 0)
 
 
 def finish(product_in, subspace_in, product, subspace, sem):
@@ -271,8 +258,13 @@
     count, _, blk, _ = vectors.shape
     width = left_environment_blocks.shape[1]
     sectors = lax.axis_size("sector")
-    group = 2 if width % 2 == 0 else 1
-    steps = width // group
+    group = []
+    first = 0
+    while first < width:
+        size = max(1, (width - first) // 2)
+        group.append((first, size))
+        first += size
+    steps = len(group)
     tile_rows = -(-count * count // 8) * 8
     vmem = pl.BlockSpec(memory_space=pltpu.VMEM)
     hbm = pl.BlockSpec(memory_space=pltpu.HBM)

time: 52 us -> 51.8 us (level)
  no operation moved by 1% of the time
where the time goes in v4:
time: 51.8 us; the launch traced here: 51.7 us
  Pallas kernels  51 us (98%)
  between operations  0.64 us (1%)
    pallas_call x1, Pallas kernels, shards(): pl.pallas_call(functools.partial(kernel, sectors, group), out_shape=(jax....  49.4 us
    pallas_call x1, Pallas kernels, shards(): pl.pallas_call(finish, out_shape=(jax.ShapeDtypeStruct(product.shape, pro...  1.67 us

profile of v4, /device:TPU:0, one launch (start us, length us, event | category | flops | bytes accessed | tf_op | source)
XLA Modules:
  0.0 51.7 jit_solution(2284150423071923902)
XLA Ops:
  0.6 49.4 %shard_map.86 = (bf16[2,1,256,256]{3,2,1,0:T(8,128)(2,1)}, f32[2,2]{1,0:T(2,128)}) custom-call(s32[16]{0:T(128)} %left_sizes_in.1, s32[16]{0:T(128)} %right_sizes_in.1, f32[26,26]{1,0:T(8,128)} %coef_in.1, s32[26,26]{1,0:T(8,128)} %pattern_in.1, bf16[2,1,256,256]{3,2,1,0:T(8,128)(2,1)} %vectors_in.1, bf16[1,26,256,256]{3,2,1,0:T(8,128)(2,1)} %left_env.1, ...), custom_call_target="tpu_custom_call" | custom-call | flops 3489660928 | bytes 10223616 | tf_op jit(solution)/shard_map/pallas_call | solution.py:271
  50.0 1.7 %shard_map.87 = (bf16[2,1,256,256]{3,2,1,0:T(8,128)(2,1)}, f32[2,2]{1,0:T(2,128)}) custom-call(bf16[2,1,256,256]{3,2,1,0:T(8,128)(2,1)} %get-tuple-element.4.product_in, f32[2,2]{1,0:T(2,128)} %get-tuple-element.5.subspace_in), custom_call_target="tpu_custom_call" | custom-call | tf_op jit(solution)/shard_map/pallas_call | solution.py:318
